TPU v7x, 32 devices: a whole 2x2x4 slice. The times are simulated.
32 devices in a mesh: dp: 16 (over z, x, core), sub: 2 (over y).
Axes of the slice: x: 2, y: 2, z: 4, core: 2. Of those that a mesh axis runs over, the one named last changes fastest.
Arguments:
- picture_encoder_embeds: float32 [4096, 1152], P(('dp', 'sub')), may hold values from -0.24 to 0.24
- caption_encoder_embeds: float32 [4096, 1152], P(('dp', 'sub')), may hold values from -0.24 to 0.24
- score_multiplier: float32 [], replicated, may hold values from 2 to 10
- score_offset_term: float32 [], replicated, may hold values from -4 to -1
Outputs:
- image_grad: float32 [4096, 1152], P(('dp', 'sub'))
- text_grad: float32 [4096, 1152], P(('dp', 'sub'))
All inputs are finite; a program needn't handle non-finite values.
Results may differ from a plain program's by a relative error of at most 0.005.
Values may be sent and summed in bfloat16 or wider, within the bound.
A program may use at most 64 MiB of HBM per device.

v0:
```python
import functools

import jax
import jax.numpy as jnp
from jax import lax
from jax.experimental import pallas as pl
from jax.experimental.pallas import tpu as pltpu
from jax.sharding import PartitionSpec as P

PIECES = 4
EARLY = 3
NT = (((1,), (1,)), ((), ()))
TN = (((0,), (0,)), ((), ()))


def dot(a, b, dims):
    return lax.dot_general(a, b, dims, preferred_element_type=jnp.float32)


def inverse_norm(values):
    return lax.rsqrt(jnp.sum(values * values, axis=-1, keepdims=True) + 1e-06)


def backward_norm(values, inverse, direction):
    unit = values * inverse
    return (direction - unit * jnp.sum(unit * direction, axis=-1, keepdims=True)) * inverse


def kernel(
    groups, rows,
    scale_ref, offset_ref, image_hbm, text_hbm,
    image_out, text_out,
    image_x, text_x, image_inv, text_inv,
    image_low, text_low, coef, partner_coef,
    image_part, text_part,
    image_send, mate_send, ext_send,
    image_recv, mate_recv, ext_recv,
    load_sem, send_sem, recv_sem, turn,
):
    g = lax.axis_index("dp")
    s = lax.axis_index("sub")
    odd = lax.rem(g, 2)
    mate = g + 1 - 2 * odd
    ext = lax.rem(g - 1 + 2 * odd + groups, groups)
    partner = (g, 1 - s)
    mate_id = (mate, s)
    ext_id = (ext, s)

    wrap = jnp.logical_or(g == 0, g == groups - 1)
    near = jnp.logical_and(lax.rem((g + 1) // 2, 2) == 1, g != groups - 2)
    leads = jnp.logical_or(near, wrap)
    hands_over = jnp.logical_and(leads, g > 1)

    step = rows // PIECES
    pieces = [pl.ds(c * step, step) for c in range(PIECES)]

    barrier = pltpu.get_barrier_semaphore()
    for who in (partner, mate_id, ext_id):
        pl.semaphore_signal(barrier, inc=1, device_id=who, device_id_type=pl.DeviceIdType.MESH)

    loads = []
    for c, piece in enumerate(pieces):
        pair = (
            pltpu.make_async_copy(text_hbm.at[piece], text_x.at[piece], load_sem.at[0, c]),
            pltpu.make_async_copy(image_hbm.at[piece], image_x.at[piece], load_sem.at[1, c]),
        )
        for copy in pair:
            copy.start()
        loads.append(pair)

    def remote(src, dst, kind, c, who):
        return pltpu.make_async_remote_copy(
            src_ref=src,
            dst_ref=dst,
            send_sem=send_sem.at[kind, c],
            recv_sem=recv_sem.at[kind, c],
            device_id=who,
            device_id_type=pl.DeviceIdType.MESH,
        )

    def send(*args):
        copy = remote(*args)
        copy.start()
        return copy

    ext_text, mate_text, partner_image = [], [], []
    for c, piece in enumerate(pieces):
        loads[c][0].wait()
        values = text_x[piece, :]
        inverse = inverse_norm(values)
        text_inv[piece, :] = inverse
        text_low[piece, :] = (values * inverse).astype(jnp.bfloat16)
        if c == 0:
            pl.semaphore_wait(barrier, 3)
        own = text_low.at[piece]
        ext_text.append(remote(own, text_low.at[pl.ds(2 * rows + c * step, step)], 0, c, ext_id))
        pl.when(leads)(ext_text[c].start)
        mate_text.append(send(own, text_low.at[pl.ds(rows + c * step, step)], 1, c, mate_id))
        loads[c][1].wait()
        values = image_x[piece, :]
        inverse = inverse_norm(values)
        image_inv[piece, :] = inverse
        image_low[piece, :] = (values * inverse).astype(jnp.bfloat16)
        own = image_low.at[piece]
        partner_image.append(remote(own, image_low.at[pl.ds(rows + c * step, step)], 2, c, partner))
        pl.when(leads)(partner_image[c].start)

    scale = scale_ref[0, 0]
    offset = offset_ref[0, 0]

    def fill(text_at, text_rows, image_at, image_rows, diagonal=False):
        texts = pl.ds(text_at, text_rows)
        images = pl.ds(image_at, image_rows)
        scores = scale * dot(text_low[texts, :], image_low[images, :], NT) + offset
        if diagonal:
            row = lax.broadcasted_iota(jnp.int32, scores.shape, 0)
            col = lax.broadcasted_iota(jnp.int32, scores.shape, 1)
            label = jnp.where(row == col, jnp.float32(1.0), jnp.float32(-1.0))
            values = -label * scale * (1.0 / (1.0 + jnp.exp(label * scores)))
        else:
            values = scale * (1.0 / (1.0 + jnp.exp(-scores)))
        coef[texts, images] = values.astype(jnp.bfloat16)

    def terms(texts):
        return jnp.dot(coef[texts, :], image_low[...], preferred_element_type=jnp.float32)

    fill(0, rows, 0, rows, diagonal=True)

    @pl.when(hands_over)
    def _():
        for c in range(EARLY):
            ext_text[c].wait_send()
            partner_image[c].wait_send()
        pl.semaphore_signal(
            turn, inc=1, device_id=mate_id, device_id_type=pl.DeviceIdType.MESH
        )

    @pl.when(jnp.logical_not(leads))
    def _():
        pl.semaphore_wait(turn, 1)
        for c in range(PIECES):
            ext_text[c].start()
            partner_image[c].start()

    for copy in mate_text:
        copy.wait_recv()
    fill(rows, rows, 0, rows)
    for copy in partner_image:
        copy.wait_recv()
    fill(0, 2 * rows, rows, rows)
    for copy in ext_text:
        copy.wait_recv()
    fill(2 * rows, rows, 0, 2 * rows)
    partner_coef[...] = coef[:, rows:].T

    ext_send[...] = terms(pl.ds(2 * rows, rows)).astype(jnp.bfloat16)
    ext_terms = [
        send(ext_send.at[piece], ext_recv.at[piece], 3, c, ext_id)
        for c, piece in enumerate(pieces)
    ]
    image_send[...] = jnp.dot(
        partner_coef[...], text_low[...], preferred_element_type=jnp.float32
    ).astype(jnp.bfloat16)
    image_terms = [
        send(image_send.at[piece], image_recv.at[piece], 5, c, partner)
        for c, piece in enumerate(pieces)
    ]
    near_terms = terms(pl.ds(0, 2 * rows))
    mate_send[...] = near_terms[rows:].astype(jnp.bfloat16)
    mate_terms = [
        send(mate_send.at[piece], mate_recv.at[piece], 4, c, mate_id)
        for c, piece in enumerate(pieces)
    ]
    text_part[...] = near_terms[:rows]
    image_part[...] = dot(coef[:, :rows], text_low[...], TN)

    for c, piece in enumerate(pieces):
        mate_terms[c].wait_recv()
        ext_terms[c].wait_recv()
        direction = (
            text_part[piece, :]
            + mate_recv[piece, :].astype(jnp.float32)
            + ext_recv[piece, :].astype(jnp.float32)
        )
        text_out[piece, :] = backward_norm(text_x[piece, :], text_inv[piece, :], direction)
        image_terms[c].wait_recv()
        direction = image_part[piece, :] + image_recv[piece, :].astype(jnp.float32)
        image_out[piece, :] = backward_norm(image_x[piece, :], image_inv[piece, :], direction)

    @pl.when(jnp.logical_not(hands_over))
    def _():
        for c in range(EARLY):
            ext_text[c].wait_send()
            partner_image[c].wait_send()

    for copies in (
        ext_text[EARLY:], partner_image[EARLY:], mate_text, ext_terms, mate_terms, image_terms
    ):
        for copy in copies:
            copy.wait_send()


def store(image_ref, text_ref, image_out, text_out, sem):
    step = image_ref.shape[0] // PIECES
    copies = []
    for c in range(PIECES):
        piece = pl.ds(c * step, step)
        copies += [
            pltpu.make_async_copy(image_ref.at[piece], image_out.at[piece], sem.at[0, c]),
            pltpu.make_async_copy(text_ref.at[piece], text_out.at[piece], sem.at[1, c]),
        ]
    for copy in copies:
        copy.start()
    for copy in copies:
        copy.wait()


def shards(groups, image, text, scale, offset):
    rows, width = image.shape
    full = pltpu.VMEM
    f32, low = jnp.float32, jnp.bfloat16
    image = pltpu.with_memory_space_constraint(image, pltpu.HBM)
    text = pltpu.with_memory_space_constraint(text, pltpu.HBM)
    grads = pl.pallas_call(
        functools.partial(kernel, groups, rows),
        out_shape=(jax.ShapeDtypeStruct((rows, width), f32),) * 2,
        in_specs=[pl.BlockSpec(memory_space=pltpu.SMEM)] * 2
        + [pl.BlockSpec(memory_space=pltpu.HBM)] * 2,
        out_specs=(pl.BlockSpec(memory_space=pltpu.VMEM),) * 2,
        scratch_shapes=[
            full((rows, width), f32),
            full((rows, width), f32),
            full((rows, 1), f32),
            full((rows, 1), f32),
            full((2 * rows, width), low),
            full((3 * rows, width), low),
            full((3 * rows, 2 * rows), low),
            full((rows, 3 * rows), low),
            full((rows, width), f32),
            full((rows, width), f32),
        ]
        + [full((rows, width), low)] * 6
        + [
            pltpu.SemaphoreType.DMA((2, PIECES)),
            pltpu.SemaphoreType.DMA((6, PIECES)),
            pltpu.SemaphoreType.DMA((6, PIECES)),
            pltpu.SemaphoreType.REGULAR,
        ],
        compiler_params=pltpu.CompilerParams(
            collective_id=0, has_side_effects=True, vmem_limit_bytes=32 * 1024 * 1024
        ),
        cost_estimate=pl.CostEstimate(
            flops=36 * rows * rows * width,
            bytes_accessed=16 * rows * width,
            transcendentals=6 * rows * rows,
        ),
    )(scale.reshape(1, 1), offset.reshape(1, 1), image, text)
    return tuple(
        pl.pallas_call(
            store,
            out_shape=(jax.ShapeDtypeStruct((rows, width), f32),) * 2,
            in_specs=[pl.BlockSpec(memory_space=pl.ANY)] * 2,
            out_specs=(pl.BlockSpec(memory_space=pltpu.HBM),) * 2,
            scratch_shapes=[pltpu.SemaphoreType.DMA((2, PIECES))],
            compiler_params=pltpu.CompilerParams(vmem_limit_bytes=16 * 1024 * 1024),
        )(*grads)
    )


def solution(mesh):
    if mesh.shape["sub"] != 2 or mesh.shape["dp"] % 4 or mesh.shape["dp"] < 4:
        raise ValueError("unsupported mesh")
    placed = (P(("dp", "sub"), None), P(("dp", "sub"), None), P(), P())
    return jax.shard_map(
        functools.partial(shards, mesh.shape["dp"]),
        mesh=mesh,
        in_specs=placed,
        out_specs=(P(("dp", "sub"), None), P(("dp", "sub"), None)),
        check_vma=False,
    )
```

profile of v0, /device:TPU:0, one launch (start us, length us, event | category | flops | bytes accessed | tf_op | source)
XLA Modules:
  0.0 25.2 jit_solution(10637344669147979144)
XLA Ops:
  1.9 22.2 %shard_map.59 = (f32[128,1152]{1,0:T(8,128)S(1)}, f32[128,1152]{1,0:T(8,128)S(1)}) custom-call(f32[1,1]{1,0:T(1,128)} %bitcast.2.scale_ref, f32[1,1]{1,0:T(1,128)} %bitcast.3.offset_ref, f32[128,1152]{1,0:T(8,128)} %image_hbm.1, f32[128,1152]{1,0:T(8,128)} %text_hbm.1), custom_call_target="tpu_custom_call" | custom-call | flops 679477248 | bytes 2359296 | tf_op jit(solution)/shard_map/pallas_call | solution.py:224
  24.1 1.1 %shard_map.60 = (f32[128,1152]{1,0:T(8,128)}, f32[128,1152]{1,0:T(8,128)}) custom-call(f32[128,1152]{1,0:T(8,128)S(1)} %get-tuple-element.4.image_ref, f32[128,1152]{1,0:T(8,128)S(1)} %get-tuple-element.5.text_ref), custom_call_target="tpu_custom_call" | custom-call | tf_op jit(solution)/shard_map/pallas_call | solution.py:259
where the time goes:
time: 25.3 us; the launch traced here: 25.2 us
  Pallas kernels  23.3 us (92%)
  between operations  1.93 us (8%)
    pallas_call x1, Pallas kernels, shards(): pl.pallas_call(functools.partial(kernel, groups, rows), out_shape=(jax.Sh...  22.2 us
    pallas_call x1, Pallas kernels, shards(): pl.pallas_call(store, out_shape=(jax.ShapeDtypeStruct((rows, width), f32)...  1.07 us

commit v1 on v0

--- a/solution.py
+++ b/solution.py
@@ -28,14 +28,15 @@
 
 def kernel(
     groups, rows,
-    scale_ref, offset_ref, image_hbm, text_hbm,
+    scale_hbm, offset_hbm, image_hbm, text_hbm,
     image_out, text_out,
     image_x, text_x, image_inv, text_inv,
     image_low, text_low, coef, partner_coef,
     image_part, text_part,
     image_send, mate_send, ext_send,
     image_recv, mate_recv, ext_recv,
-    load_sem, send_sem, recv_sem, turn,
+    scale_ref, offset_ref,
+    load_sem, scalar_sem, send_sem, recv_sem, turn, later_turn,
 ):
     g = lax.axis_index("dp")
     s = lax.axis_index("sub")
@@ -58,6 +59,10 @@
     for who in (partner, mate_id, ext_id):
         pl.semaphore_signal(barrier, inc=1, device_id=who, device_id_type=pl.DeviceIdType.MESH)
 
+    scalars = [
+        pltpu.make_async_copy(scale_hbm, scale_ref, scalar_sem.at[0]),
+        pltpu.make_async_copy(offset_hbm, offset_ref, scalar_sem.at[1]),
+    ]
     loads = []
     for c, piece in enumerate(pieces):
         pair = (
@@ -67,6 +72,9 @@
         for copy in pair:
             copy.start()
         loads.append(pair)
+
+    for copy in scalars:
+        copy.start()
 
     def remote(src, dst, kind, c, who):
         return pltpu.make_async_remote_copy(
@@ -105,6 +113,8 @@
         partner_image.append(remote(own, image_low.at[pl.ds(rows + c * step, step)], 2, c, partner))
         pl.when(leads)(partner_image[c].start)
 
+    for copy in scalars:
+        copy.wait()
     scale = scale_ref[0, 0]
     offset = offset_ref[0, 0]
 
@@ -155,9 +165,15 @@
 
     ext_send[...] = terms(pl.ds(2 * rows, rows)).astype(jnp.bfloat16)
     ext_terms = [
-        send(ext_send.at[piece], ext_recv.at[piece], 3, c, ext_id)
+        remote(ext_send.at[piece], ext_recv.at[piece], 3, c, ext_id)
         for c, piece in enumerate(pieces)
     ]
+
+    @pl.when(g != groups - 2)
+    def _():
+        for copy in ext_terms:
+            copy.start()
+
     image_send[...] = jnp.dot(
         partner_coef[...], text_low[...], preferred_element_type=jnp.float32
     ).astype(jnp.bfloat16)
@@ -174,6 +190,20 @@
     text_part[...] = near_terms[:rows]
     image_part[...] = dot(coef[:, :rows], text_low[...], TN)
 
+    @pl.when(g == groups - 1)
+    def _():
+        for copy in ext_terms[:EARLY]:
+            copy.wait_send()
+        pl.semaphore_signal(
+            later_turn, inc=1, device_id=mate_id, device_id_type=pl.DeviceIdType.MESH
+        )
+
+    @pl.when(g == groups - 2)
+    def _():
+        pl.semaphore_wait(later_turn, 1)
+        for copy in ext_terms:
+            copy.start()
+
     for c, piece in enumerate(pieces):
         mate_terms[c].wait_recv()
         ext_terms[c].wait_recv()
@@ -193,8 +223,14 @@
             ext_text[c].wait_send()
             partner_image[c].wait_send()
 
+    @pl.when(g != groups - 1)
+    def _():
+        for copy in ext_terms[:EARLY]:
+            copy.wait_send()
+
     for copies in (
-        ext_text[EARLY:], partner_image[EARLY:], mate_text, ext_terms, mate_terms, image_terms
+        ext_text[EARLY:], partner_image[EARLY:], mate_text,
+        ext_terms[EARLY:], mate_terms, image_terms,
     ):
         for copy in copies:
             copy.wait_send()
@@ -219,13 +255,14 @@
     rows, width = image.shape
     full = pltpu.VMEM
     f32, low = jnp.float32, jnp.bfloat16
+    scale = scale.reshape(1, 1)
+    offset = offset.reshape(1, 1)
     image = pltpu.with_memory_space_constraint(image, pltpu.HBM)
     text = pltpu.with_memory_space_constraint(text, pltpu.HBM)
     grads = pl.pallas_call(
         functools.partial(kernel, groups, rows),
         out_shape=(jax.ShapeDtypeStruct((rows, width), f32),) * 2,
-        in_specs=[pl.BlockSpec(memory_space=pltpu.SMEM)] * 2
-        + [pl.BlockSpec(memory_space=pltpu.HBM)] * 2,
+        in_specs=[pl.BlockSpec(memory_space=pltpu.HBM)] * 4,
         out_specs=(pl.BlockSpec(memory_space=pltpu.VMEM),) * 2,
         scratch_shapes=[
             full((rows, width), f32),
@@ -241,9 +278,13 @@
         ]
         + [full((rows, width), low)] * 6
         + [
+            pltpu.SMEM((1, 1), f32),
+            pltpu.SMEM((1, 1), f32),
             pltpu.SemaphoreType.DMA((2, PIECES)),
+            pltpu.SemaphoreType.DMA((2,)),
             pltpu.SemaphoreType.DMA((6, PIECES)),
             pltpu.SemaphoreType.DMA((6, PIECES)),
+            pltpu.SemaphoreType.REGULAR,
             pltpu.SemaphoreType.REGULAR,
         ],
         compiler_params=pltpu.CompilerParams(
@@ -254,7 +295,7 @@
             bytes_accessed=16 * rows * width,
             transcendentals=6 * rows * rows,
         ),
-    )(scale.reshape(1, 1), offset.reshape(1, 1), image, text)
+    )(scale, offset, image, text)
     return tuple(
         pl.pallas_call(
             store,

time: 25.3 us -> 25.4 us (level)
  no operation moved by 1% of the time
where the time goes in v1:
time: 25.4 us; the launch traced here: 25.2 us
  Pallas kernels  23.3 us (92%)
  between operations  1.93 us (8%)
    pallas_call x1, Pallas kernels, shards(): pl.pallas_call(functools.partial(kernel, groups, rows), out_shape=(jax.Sh...  22.2 us
    pallas_call x1, Pallas kernels, shards(): pl.pallas_call(store, out_shape=(jax.ShapeDtypeStruct((rows, width), f32)...  1.07 us

profile of v1, /device:TPU:0, one launch (start us, length us, event | category | flops | bytes accessed | tf_op | source)
XLA Modules:
  0.0 25.2 jit_solution(13490796218541077551)
XLA Ops:
  1.9 22.2 %shard_map.59 = (f32[128,1152]{1,0:T(8,128)S(1)}, f32[128,1152]{1,0:T(8,128)S(1)}) custom-call(f32[1,1]{1,0:T(1,128)} %bitcast.2.scale_hbm, f32[1,1]{1,0:T(1,128)} %bitcast.3.offset_hbm, f32[128,1152]{1,0:T(8,128)} %image_hbm.1, f32[128,1152]{1,0:T(8,128)} %text_hbm.1), custom_call_target="tpu_custom_call" | custom-call | flops 679477248 | bytes 2359296 | tf_op jit(solution)/shard_map/pallas_call | solution.py:262
  24.1 1.1 %shard_map.60 = (f32[128,1152]{1,0:T(8,128)}, f32[128,1152]{1,0:T(8,128)}) custom-call(f32[128,1152]{1,0:T(8,128)S(1)} %get-tuple-element.4.image_ref, f32[128,1152]{1,0:T(8,128)S(1)} %get-tuple-element.5.text_ref), custom_call_target="tpu_custom_call" | custom-call | tf_op jit(solution)/shard_map/pallas_call | solution.py:300

commit v2 on v0

--- a/solution.py
+++ b/solution.py
@@ -8,7 +8,7 @@
 from jax.sharding import PartitionSpec as P
 
 PIECES = 4
-EARLY = 3
+EARLY = 2
 NT = (((1,), (1,)), ((), ()))
 TN = (((0,), (0,)), ((), ()))
 
@@ -46,9 +46,7 @@
     mate_id = (mate, s)
     ext_id = (ext, s)
 
-    wrap = jnp.logical_or(g == 0, g == groups - 1)
-    near = jnp.logical_and(lax.rem((g + 1) // 2, 2) == 1, g != groups - 2)
-    leads = jnp.logical_or(near, wrap)
+    leads = jnp.logical_or(lax.rem((g + 1) // 2, 2) == 0, g == 1)
     hands_over = jnp.logical_and(leads, g > 1)
 
     step = rows // PIECES

time: 25.3 us -> 25.9 us (1.024)
  the two profiles are of different devices: /device:TPU:0 before, /device:TPU:1 now
where the time goes in v2:
time: 25.9 us; the launch traced here: 25.7 us
  Pallas kernels  23.8 us (92%)
  between operations  1.93 us (7%)
    pallas_call x1, Pallas kernels, shards(): pl.pallas_call(functools.partial(kernel, groups, rows), out_shape=(jax.Sh...  22.7 us
    pallas_call x1, Pallas kernels, shards(): pl.pallas_call(store, out_shape=(jax.ShapeDtypeStruct((rows, width), f32)...  1.07 us

profile of v2, /device:TPU:1, one launch (start us, length us, event | category | flops | bytes accessed | tf_op | source)
XLA Modules:
  0.0 25.7 jit_solution(8540575608985922066)
XLA Ops:
  1.9 22.7 %shard_map.59 = (f32[128,1152]{1,0:T(8,128)S(1)}, f32[128,1152]{1,0:T(8,128)S(1)}) custom-call(f32[1,1]{1,0:T(1,128)} %bitcast.2.scale_ref, f32[1,1]{1,0:T(1,128)} %bitcast.3.offset_ref, f32[128,1152]{1,0:T(8,128)} %image_hbm.1, f32[128,1152]{1,0:T(8,128)} %text_hbm.1), custom_call_target="tpu_custom_call" | custom-call | flops 679477248 | bytes 2359296 | tf_op jit(solution)/shard_map/pallas_call | solution.py:222
  24.7 1.1 %shard_map.60 = (f32[128,1152]{1,0:T(8,128)}, f32[128,1152]{1,0:T(8,128)}) custom-call(f32[128,1152]{1,0:T(8,128)S(1)} %get-tuple-element.4.image_ref, f32[128,1152]{1,0:T(8,128)S(1)} %get-tuple-element.5.text_ref), custom_call_target="tpu_custom_call" | custom-call | tf_op jit(solution)/shard_map/pallas_call | solution.py:257
